TPU v7x, 256 devices: a whole 4x4x8 slice. The times are simulated.
256 devices in a mesh: space: 32 (over z, x), tm: 8 (over y, core).
Axes of the slice: x: 4, y: 4, z: 8, core: 2. Of those that a mesh axis runs over, the one named last changes fastest.
Arguments:
- snapshots: bfloat16 [512, 1048576], P('tm', 'space'), may hold values from -6 to 6
- pod_basis: bfloat16 [68, 1048576], P(None, 'space'), may hold values from -0.005859375 to 0.005859375
- penalty: float32 [2415], replicated, may hold values from 0.05 to 1
Outputs:
- normal: float32 [2416, 2415], P('tm')
- rhs: float32 [2416, 68], P('tm')
- reduced_state: float32 [8, 64, 68], P('tm', 'space')
- state_rates: float32 [8, 64, 68], P('tm', 'space')
All inputs are finite; a program needn't handle non-finite values.
Results may differ from a plain program's by a relative error of at most 0.0003.
Values may be sent and summed in bfloat16 or wider, within the bound.
A program may use at most 128 MiB of HBM per device.

v0:
```python
import jax
import jax.numpy as jnp
import numpy as np
from jax import lax
from jax.sharding import Mesh
from jax.sharding import PartitionSpec as P

TM = ("tm_0", "tm_1")
SPACE = ("space_0", "space_1")


def padded_2(block, sides, width):
    for axis, dim in sides:
        count = lax.axis_size(axis)
        forward = [(i, i + 1) for i in range(count - 1)]
        backward = [(target, source) for source, target in forward]
        low = lax.ppermute(
            lax.slice_in_dim(block, block.shape[dim] - width, None, axis=dim), axis, forward
        )
        high = lax.ppermute(lax.slice_in_dim(block, 0, width, axis=dim), axis, backward)
        block = jnp.concatenate([low, block, high], axis=dim)
    return block


def cut_along(shard, dim, devices):
    dims = shard.shape
    parts = shard.reshape(*dims[:dim], devices, dims[dim] // devices, *dims[dim + 1 :])
    return jnp.moveaxis(parts, dim, 0)


def sent_and_summed(shard, axis, dim):
    parts = cut_along(shard, dim, lax.axis_size(axis))
    arrived = lax.all_to_all(parts, axis, split_axis=0, concat_axis=0, tiled=True)
    return arrived.sum(axis=0)


def side_by_side(arrays, axis, dim, along):
    both = jnp.concatenate(arrays, axis=along)
    out, at, done = (sent_and_summed(both, axis, dim), 0, [])
    for a in arrays:
        done.append(lax.slice_in_dim(out, at, at + a.shape[along], axis=along))
        at += a.shape[along]
    return tuple(done)


def sent_to_all(shard, axis):
    copies = jnp.broadcast_to(shard, (lax.axis_size(axis), *shard.shape))
    return lax.all_to_all(copies, axis, split_axis=0, concat_axis=0, tiled=True)


def in_order(parts, dim):
    parts = jnp.moveaxis(parts, 0, dim)
    dims = parts.shape
    return parts.reshape(*dims[:dim], dims[dim] * dims[dim + 1], *dims[dim + 2 :])


def gathered_by_axis(shard, axes, dim):
    far, near = axes
    parts = sent_to_all(sent_to_all(shard, far), near)
    return in_order(parts.swapaxes(0, 1).reshape(-1, *shard.shape), dim)


def in_one_piece(arrays, axis, dim, along):
    widths = [a.shape[along] for a in arrays]
    both = jnp.concatenate(arrays, axis=along)
    out = gathered_by_axis(both, axis, dim)
    return tuple(jnp.split(out, [sum(widths[:k]) for k in range(1, len(widths))], axis=along))


def features(reduced):
    rows_count, mode_count = reduced.shape
    upper_rows, upper_cols = np.triu_indices(mode_count)
    flat_index = (upper_rows * mode_count + upper_cols).astype(np.int32)
    outer_prod = (reduced[:, :, None] * reduced[:, None, :]).reshape(
        rows_count, mode_count * mode_count
    )
    quadratic = jnp.take(outer_prod, flat_index, axis=1)
    constant = jnp.ones((rows_count, 1), jnp.float32)
    return jnp.concatenate([constant, reduced, quadratic], axis=1)


def project(rows_in, pod_basis):
    return lax.dot_general(
        rows_in, pod_basis, (((1,), (1,)), ((), ())), preferred_element_type=jnp.float32
    )


def normal_block(feature_all, rates_all, first_row, block_width):
    padded = jnp.pad(feature_all, ((0, 0), (0, block_width)))
    columns = lax.dynamic_slice_in_dim(padded, first_row, block_width, 1)
    dims = (((0,), (0,)), ((), ()))
    gram_part = lax.dot_general(
        columns,
        feature_all,
        dims,
        precision=lax.Precision.HIGHEST,
        preferred_element_type=jnp.float32,
    )
    rhs_part = lax.dot_general(
        columns,
        rates_all,
        dims,
        precision=lax.Precision.HIGHEST,
        preferred_element_type=jnp.float32,
    )
    return (gram_part, rhs_part)


def shards(snapshots, pod_basis, penalty):
    tm_index = lax.axis_index(TM)
    tm_count = lax.axis_size(TM)
    partial_value = project(snapshots, pod_basis)
    extended = padded_2(partial_value, ((TM, 0),), 1)
    own_part = extended[1:-1]
    centred = (extended[2:] - extended[:-2]) * 0.5
    first_rate = jnp.where(tm_index == 0, extended[2] - extended[1], centred[0])
    last_rate = jnp.where(tm_index == tm_count - 1, extended[-2] - extended[-3], centred[-1])
    rate_part = jnp.concatenate([first_rate[None], centred[1:-1], last_rate[None]], axis=0)
    reduced, rate_rows = side_by_side((own_part, rate_part), SPACE, 0, 1)
    feat_width = penalty.shape[0]
    padded_width = feat_width + (tm_count - feat_width % tm_count) % tm_count
    block_width = padded_width // tm_count
    first_row = tm_index * block_width
    total_snaps = snapshots.shape[0] * tm_count
    every_state, every_rates = in_one_piece(
        (reduced, rate_rows), (("space_0", "space_1"), ("tm_0", "tm_1")), 0, 1
    )
    gram_sum, rhs_sum = normal_block(features(every_state), every_rates, first_row, block_width)
    row_global = first_row + lax.iota(jnp.int32, block_width)
    col_global = lax.iota(jnp.int32, feat_width)
    penalty_pad = jnp.pad(penalty, (0, block_width))
    penalty_rows = lax.dynamic_slice_in_dim(penalty_pad, first_row, block_width, 0)
    on_diagonal = row_global[:, None] == col_global[None, :]
    normal = gram_sum / total_snaps + jnp.where(on_diagonal, penalty_rows[:, None], 0.0)
    rhs = rhs_sum / total_snaps
    return (normal, rhs, reduced[None], rate_rows[None])


def solution(mesh):
    split = Mesh(mesh.devices.reshape(8, 4, 4, 2), ("space_0", "space_1", "tm_0", "tm_1"))
    placed = (P(TM, SPACE), P(None, SPACE), P())
    return jax.shard_map(
        shards,
        mesh=split,
        in_specs=placed,
        out_specs=(P(TM, None), P(TM, None), P(TM, SPACE, None), P(TM, SPACE, None)),
        check_vma=False,
    )
```

profile of v0, /device:TPU:1, one launch (start us, length us, event | category | flops | bytes accessed | tf_op | source)
XLA Modules:
  0.0 119.1 jit_solution(13422560093779277588)
XLA Ops:
  0.6 0.0 copy-start.1
  0.6 0.0 copy-start.2
  0.7 5.0 %fusion.9 = f32[64,68]{1,0:T(8,128)S(1)} fusion(bf16[64,32768]{1,0:T(8,128)(2,1)} %param.4, bf16[68,32768]{1,0:T(8,128)(2,1)} %param.5), kind=kOutput, calls=%fused_computation.27 | convolution fusion | flops 285212672 | bytes 8668160 | tf_op jit(solution)/shard_map/dot_general | solution.py:83
  5.7 5.1 %collective-permute-start = (f32[1,68]{1,0:T(1,128)S(1)}, f32[1,68]{1,0:T(1,128)S(1)}, u32[]{:S(2)}, u32[]{:S(2)}) collective-permute-start(f32[1,68]{1,0:T(1,128)S(1)} %get-tuple-element.6), channel_id=1, source_target_pairs={{1,0},{2,1},{3,2},{4,3},{5,4},{6,5},{7,6},{9,8},{10,9},{11,10},{12... | collective-permute-start | bytes 824 | tf_op jit(solution)/shard_map/ppermute | solution.py:20
  10.8 1.9 %collective-permute-start.1 = (f32[1,68]{1,0:T(1,128)S(1)}, f32[1,68]{1,0:T(1,128)S(1)}, u32[]{:S(2)}, u32[]{:S(2)}) collective-permute-start(f32[1,68]{1,0:T(1,128)S(1)} %get-tuple-element.7), channel_id=1, source_target_pairs={{0,1},{1,2},{2,3},{3,4},{4,5},{5,6},{6,7},{8,9},{9,10},{10,11},{11... | collective-permute-start | bytes 824 | tf_op jit(solution)/shard_map/ppermute | solution.py:17
  12.8 0.0 collective-permute-done
  12.8 1.1 collective-permute-done.1
  13.9 0.1 maximum_maximum_fusion
  14.0 0.7 reshape.27
  14.6 10.1 %all-to-all-start = ((f32[32,2,136]{2,1,0:T(2,128)}), f32[32,2,136]{2,1,0:T(2,128)S(1)}, u32[]{:S(2)}, u32[]{:S(2)}) async-start(f32[32,2,136]{2,1,0:T(2,128)} %reshape.27), calls=%async_computation | async-start | bytes 131072 | tf_op jit(solution)/shard_map/all_to_all | solution.py:33
  24.7 0.0 copy-done.1
  24.8 9.2 %all-to-all-done = f32[32,2,136]{2,1,0:T(2,128)S(1)} async-done(((f32[32,2,136]{2,1,0:T(2,128)}), f32[32,2,136]{2,1,0:T(2,128)S(1)}, u32[]{:S(2)}, u32[]{:S(2)}) %all-to-all-start) | async-done | bytes 34848 | tf_op jit(solution)/shard_map/all_to_all | solution.py:33
  34.0 0.7 broadcast_in_dim.47
  34.7 3.9 %all-to-all-start.1 = ((f32[32,2,136]{2,1,0:T(2,128)}), f32[32,2,136]{2,1,0:T(2,128)S(1)}, u32[]{:S(2)}, u32[]{:S(2)}) async-start(f32[32,2,136]{2,1,0:T(2,128)} %broadcast_in_dim.47), calls=%async_computation.1 | async-start | bytes 131072 | tf_op jit(solution)/shard_map/all_to_all | solution.py:48
  38.5 8.9 %all-to-all-done.1 = f32[32,2,136]{2,1,0:T(2,128)S(1)} async-done(((f32[32,2,136]{2,1,0:T(2,128)}), f32[32,2,136]{2,1,0:T(2,128)S(1)}, u32[]{:S(2)}, u32[]{:S(2)}) %all-to-all-start.1) | async-done | bytes 34848 | tf_op jit(solution)/shard_map/all_to_all | solution.py:48
  47.4 0.9 broadcast_in_dim.48
  48.3 7.7 %all-to-all-start.2 = ((f32[8,32,2,136]{3,2,1,0:T(2,128)}), f32[8,32,2,136]{3,2,1,0:T(2,128)S(1)}, u32[]{:S(2)}, u32[]{:S(2)}) async-start(f32[8,32,2,136]{3,2,1,0:T(2,128)} %broadcast_in_dim.48), calls=%async_computation.2 | async-start | bytes 1048576 | tf_op jit(solution)/shard_map/all_to_all | solution.py:48
  56.1 0.0 copy-done.2
  56.1 0.1 pad_dynamic-slice_fusion.3
  56.1 0.6 slice_bitcast_fusion
  56.8 8.8 %all-to-all-done.2 = f32[8,32,2,136]{3,2,1,0:T(2,128)S(1)} async-done(((f32[8,32,2,136]{3,2,1,0:T(2,128)}), f32[8,32,2,136]{3,2,1,0:T(2,128)S(1)}, u32[]{:S(2)}, u32[]{:S(2)}) %all-to-all-start.2) | async-done | bytes 278560 | tf_op jit(solution)/shard_map/all_to_all | solution.py:48
  65.5 0.3 copy.10
  65.8 0.4 reshape_reshape.3
  66.2 0.1 copy.12
  66.3 5.2 %broadcast_multiply_fusion = f32[512,68,68]{0,2,1:T(8,128)} fusion(f32[512,68]{0,1:T(8,128)S(1)} %copy.12), kind=kLoop, calls=%fused_computation.2 | loop fusion | flops 2367488 | bytes 9609216 | tf_op jit(solution)/shard_map/mul | solution.py:74
  71.5 10.6 %mul.35 = f32[512,4624]{0,1:T(8,128)} reshape(f32[512,68,68]{0,2,1:T(8,128)} %broadcast_multiply_fusion) | data formatting | bytes 18939904 | tf_op jit(solution)/shard_map/mul | solution.py:74
  82.2 12.3 %gather_fusion = f32[2346,512]{1,0:T(8,128)} fusion(f32[512,4624]{0,1:T(8,128)} %mul.35, s32[3072]{0:T(1024)S(1)} %pad_clamp_fusion), kind=kCustom, calls=%fused_computation | custom fusion | bytes 9618600 | tf_op jit(solution)/shard_map/jit(_take)/gather | solution.py:77
  94.4 14.8 %concatenate.21 = f32[512,2415]{0,1:T(8,128)} concatenate(f32[512,1]{0,1:T(1,128)S(1)} %broadcast_in_dim.46, f32[512,68]{0,1:T(8,128)S(1)} %copy.12, f32[512,2346]{0,1:T(8,128)} %bitcast.11), dimensions={1} | concatenate | bytes 9891840 | tf_op jit(solution)/shard_map/concatenate | solution.py:79
  109.2 0.0 copy-start
  109.2 2.7 %convolution_multiply_fusion.1 = f32[302,68]{0,1:T(8,128)} fusion(f32[512,136]{1,0:T(8,128)S(1)} %reshape_reshape.3, s32[]{:T(128)S(6)} %select_n.39, f32[512,2415]{0,1:T(8,128)} %concatenate.21), kind=kOutput, calls=%fused_computation.6 | convolution fusion | flops 126193720 | bytes 5290212 | tf_op jit(solution)/shard_map/dot_general | solution.py:99
  111.9 0.0 copy-done
  111.9 7.2 %fusion = f32[302,2415]{1,0:T(8,128)} fusion(f32[512,2415]{0,1:T(8,128)S(1)} %copy-done, f32[302]{0:T(512)S(1)} %pad_dynamic-slice_fusion.3, s32[302]{0:T(512)S(1)} %iota_add_fusion, s32[]{:T(128)S(6)} %select_n.39), kind=kOutput, calls=%fused_computation.4 | convolution fusion | flops 4483920896 | bytes 12817356 | tf_op jit(solution)/shard_map/dot_general | solution.py:92
  (9 shorter events, 0.1 us)
Async XLA Ops:
  0.6 24.1 %copy-start.1 = (s32[2346]{0:T(1024)S(1)}, s32[2346]{0:T(1024)}, u32[]{:S(2)}) copy-start(s32[2346]{0:T(1024)} %constant.60) | copy-start | bytes 28156
  0.6 55.4 %copy-start.2 = (f32[2415]{0:T(1024)S(1)}, f32[2415]{0:T(1024)}, u32[]{:S(2)}) copy-start(f32[2415]{0:T(1024)} %param.6) | copy-start | bytes 28984
  5.7 7.1 %collective-permute-start = (f32[1,68]{1,0:T(1,128)S(1)}, f32[1,68]{1,0:T(1,128)S(1)}, u32[]{:S(2)}, u32[]{:S(2)}) collective-permute-start(f32[1,68]{1,0:T(1,128)S(1)} %get-tuple-element.6), channel_id=1, source_target_pairs={{1,0},{2,1},{3,2},{4,3},{5,4},{6,5},{7,6},{9,8},{10,9},{11,10},{12... | collective-permute-start | bytes 824 | tf_op jit(solution)/shard_map/ppermute | solution.py:20
  10.8 3.0 %collective-permute-start.1 = (f32[1,68]{1,0:T(1,128)S(1)}, f32[1,68]{1,0:T(1,128)S(1)}, u32[]{:S(2)}, u32[]{:S(2)}) collective-permute-start(f32[1,68]{1,0:T(1,128)S(1)} %get-tuple-element.7), channel_id=1, source_target_pairs={{0,1},{1,2},{2,3},{3,4},{4,5},{5,6},{6,7},{8,9},{9,10},{10,11},{11... | collective-permute-start | bytes 824 | tf_op jit(solution)/shard_map/ppermute | solution.py:17
  14.6 19.3 %all-to-all-start = ((f32[32,2,136]{2,1,0:T(2,128)}), f32[32,2,136]{2,1,0:T(2,128)S(1)}, u32[]{:S(2)}, u32[]{:S(2)}) async-start(f32[32,2,136]{2,1,0:T(2,128)} %reshape.27), calls=%async_computation | async-start | bytes 131072 | tf_op jit(solution)/shard_map/all_to_all | solution.py:33
  34.7 12.7 %all-to-all-start.1 = ((f32[32,2,136]{2,1,0:T(2,128)}), f32[32,2,136]{2,1,0:T(2,128)S(1)}, u32[]{:S(2)}, u32[]{:S(2)}) async-start(f32[32,2,136]{2,1,0:T(2,128)} %broadcast_in_dim.47), calls=%async_computation.1 | async-start | bytes 131072 | tf_op jit(solution)/shard_map/all_to_all | solution.py:48
  48.3 17.2 %all-to-all-start.2 = ((f32[8,32,2,136]{3,2,1,0:T(2,128)}), f32[8,32,2,136]{3,2,1,0:T(2,128)S(1)}, u32[]{:S(2)}, u32[]{:S(2)}) async-start(f32[8,32,2,136]{3,2,1,0:T(2,128)} %broadcast_in_dim.48), calls=%async_computation.2 | async-start | bytes 1048576 | tf_op jit(solution)/shard_map/all_to_all | solution.py:48
  109.2 2.7 %copy-start = (f32[512,2415]{0,1:T(8,128)S(1)}, f32[512,2415]{0,1:T(8,128)}, u32[]{:S(2)}) copy-start(f32[512,2415]{0,1:T(8,128)} %concatenate.21) | copy-start | bytes 14837764
where the time goes:
time: 120 us; the launch traced here: 119 us
  local copies, waits for them, and re-layouts  41.5 us (35%)
  starting transfers between devices  28.7 us (24%)
  waiting for transfers between devices  27.9 us (23%)
  matrix products  14.8 us (12%)
  other arithmetic  5.36 us (4%)
    all_to_all x2, waiting for transfers between devices, sent_to_all(): return lax.all_to_all(copies, axis, split_axis=0, concat_axis=0, tiled=True)  17.6 us
    concatenate x1, local copies, waits for them, and re-layouts, features(): return jnp.concatenate([constant, reduced, quadratic], axis=1)  14.8 us
    gather x1, local copies, waits for them, and re-layouts, features(): quadratic = jnp.take(outer_prod, flat_index, axis=1)  12.3 us
    all_to_all x2, starting transfers between devices, sent_to_all(): return lax.all_to_all(copies, axis, split_axis=0, concat_axis=0, tiled=True)  11.6 us
    mul x1, local copies, waits for them, and re-layouts, features(): reduced[:, :, None] * reduced[:, None, :]  10.6 us
    all_to_all x1, starting transfers between devices, sent_and_summed(): lax.all_to_all(parts, axis, split_axis=0, concat_axis=0, tiled=True)  10.1 us
    all_to_all x1, waiting for transfers between devices, sent_and_summed(): lax.all_to_all(parts, axis, split_axis=0, concat_axis=0, tiled=True)  9.2 us
    dot_general x1, matrix products, normal_block(): lax.dot_general(columns, feature_all, dims, precision=lax.Precision.HIGHE...  7.17 us
  transfers between devices with their start and end apart: 5, of which 4 were waited for; matrix products, arithmetic and copies ran while one was open for 1% of the time, Pallas kernels for 0%

commit v1 on v0

v1 whole, which is shorter than its diff:
```python
import functools

import jax
import jax.numpy as jnp
from jax import lax
from jax.experimental import pallas as pl
from jax.experimental.pallas import tpu as pltpu
from jax.sharding import PartitionSpec as P

R = 68
HALF = R // 2
F = 1 + R + R * (R + 1) // 2
ROWS = 2560
RATE_ROW = 2432
NX, NZ, NT = 4, 8, 8
CHUNKS = 8
MESH = pl.DeviceIdType.MESH
CONTRACT_LANES = (((1,), (1,)), ((), ()))


def quadratic_rows():
    starts, at = [], 1 + R
    for i in range(R):
        starts.append(at)
        at += R - i
    return starts


def project_and_share(
    snap_hbm, pod_hbm, out_ref, snap, pod, xbuf, zbuf, tbuf, load_sem, send_sem, recv_sem
):
    space, tm = lax.axis_index("space"), lax.axis_index("tm")
    z, x = space // NX, lax.rem(space, NX)
    x_peers = [(z * NX + lax.rem(x + k, NX), tm) for k in range(1, NX)]
    z_peers = [(lax.rem(z + k, NZ) * NX + x, tm) for k in range(1, NZ)]
    t_peers = [(space, lax.rem(tm + k, NT)) for k in range(1, NT)]

    width = snap_hbm.shape[1] // CHUNKS

    def loads(i):
        cols = pl.ds(i * width, width)
        return (
            pltpu.make_async_copy(snap_hbm.at[:, cols], snap.at[:, cols], load_sem.at[0, i]),
            pltpu.make_async_copy(pod_hbm.at[:, cols], pod.at[:, cols], load_sem.at[1, i]),
        )

    for i in range(CHUNKS):
        for copy in loads(i):
            copy.start()

    barrier = pltpu.get_barrier_semaphore()
    peers = z_peers + t_peers + x_peers
    for peer in peers:
        pl.semaphore_signal(barrier, inc=1, device_id=peer, device_id_type=MESH)

    total = jnp.zeros((R, snap_hbm.shape[0]), jnp.float32)
    for i in range(CHUNKS):
        for copy in loads(i):
            copy.wait()
        cols = slice(i * width, (i + 1) * width)
        total = total + lax.dot_general(
            pod[:, cols], snap[:, cols], CONTRACT_LANES, preferred_element_type=jnp.float32
        )
    packed = jnp.concatenate([total[:HALF], total[HALF:]], axis=1)

    pl.semaphore_wait(barrier, len(peers))

    def exchange(phase, buf, rank, peers):
        count = len(peers)
        for peer in peers:
            pltpu.make_async_remote_copy(
                src_ref=buf.at[rank],
                dst_ref=buf.at[rank],
                send_sem=send_sem.at[phase],
                recv_sem=recv_sem.at[phase],
                device_id=peer,
                device_id_type=MESH,
            ).start()
        slots = buf.at[pl.ds(0, count)]
        pltpu.make_async_copy(slots, slots, recv_sem.at[phase]).wait()

    xbuf[x] = packed
    exchange(0, xbuf, x, x_peers)
    zbuf[z] = (xbuf[0] + xbuf[1]) + (xbuf[2] + xbuf[3])
    exchange(1, zbuf, z, z_peers)
    tbuf[tm] = ((zbuf[0] + zbuf[1]) + (zbuf[2] + zbuf[3])) + (
        (zbuf[4] + zbuf[5]) + (zbuf[6] + zbuf[7])
    )
    exchange(2, tbuf, tm, t_peers)

    half_lane = lax.broadcasted_iota(jnp.int32, (HALF, 128), 1) < 64
    for y in range(NT // 2):
        a, b = tbuf[2 * y], tbuf[2 * y + 1]
        out_ref[y, 0:HALF] = jnp.where(half_lane, a, pltpu.roll(b, 64, 1))
        out_ref[y, HALF:R] = jnp.where(half_lane, pltpu.roll(a, 64, 1), b)

    for phase, (buf, peers) in enumerate(((xbuf, x_peers), (zbuf, z_peers), (tbuf, t_peers))):
        slots = buf.at[pl.ds(0, len(peers))]
        pltpu.make_async_copy(slots, slots, send_sem.at[phase]).wait()


def normal_equations(
    modes_ref, pen_ref, normal_ref, rhs_ref, state_ref, rate_ref, modes, rates, feat, hi, lo, own, turned, obuf, rbuf, sem
):
    space, tm = lax.axis_index("space"), lax.axis_index("tm")
    rows = normal_ref.shape[0]
    groups = modes_ref.shape[0]
    snaps = groups * 128

    modes[:, :R] = modes_ref[...]
    modes[:, R:80] = jnp.zeros((groups, 80 - R, 128), jnp.float32)
    feat[:, 0:1] = jnp.ones((groups, 1, 128), jnp.float32)
    feat[:, 1 : 1 + R] = modes[:, :R]
    for i, at in enumerate(quadratic_rows()):
        count = -(-(R - i) // 8) * 8
        feat[:, at : at + count] = modes[:, i : i + count] * modes[:, i : i + 1]
    feat[:, F:RATE_ROW] = jnp.zeros((groups, RATE_ROW - F, 128), jnp.float32)

    whole = jnp.concatenate([modes[y, :72] for y in range(groups)], axis=1)
    col = lax.broadcasted_iota(jnp.int32, (72, snaps), 1)
    first, last = col == 0, col == snaps - 1
    after = jnp.where(last, whole, pltpu.roll(whole, snaps - 1, 1))
    before = jnp.where(first, whole, pltpu.roll(whole, 1, 1))
    rate = (after - before) * jnp.where(first | last, 1.0, 0.5)
    for y in range(groups):
        rates[y, 0:72] = rate[:, y * 128 : (y + 1) * 128]
        rates[y, 72:128] = jnp.zeros((56, 128), jnp.float32)
        feat[y, RATE_ROW:ROWS] = rates[y]

    first_row = tm * rows
    padded = own.shape[0] // 2
    for y in range(groups):
        lanes = slice(y * 128, (y + 1) * 128)
        value = feat[y, pl.ds(first_row, padded)]
        high = value.astype(jnp.bfloat16)
        own[0:padded, lanes] = high
        own[padded : 2 * padded, lanes] = (value - high.astype(jnp.float32)).astype(jnp.bfloat16)

        def split(r, carry, y=y, lanes=lanes):
            at = pl.ds(pl.multiple_of(r * 64, 64), 64)
            value = feat[y, at]
            high = value.astype(jnp.bfloat16)
            hi[at, lanes] = high
            lo[at, lanes] = (value - high.astype(jnp.float32)).astype(jnp.bfloat16)
            return carry

        lax.fori_loop(0, ROWS // 64, split, 0, unroll=4)

    at = lax.rem(tm, 2) * 64 + 2 * space
    turned[0] = jnp.concatenate([modes[tm // 2], jnp.zeros((48, 128), jnp.float32)], axis=0).T
    turned[1] = rates[tm // 2].T
    state_ref[0] = turned[0, pl.ds(at, 2)][:, :R]
    rate_ref[0] = turned[1, pl.ds(at, 2)][:, :R]

    row = lax.broadcasted_iota(jnp.int32, (rows, 256), 0) + first_row
    col = lax.broadcasted_iota(jnp.int32, (rows, 256), 1)
    copies = []
    tiles = ROWS // 256
    for n in range(tiles):
        cols = slice(n * 256, (n + 1) * 256)
        both = lax.dot_general(own[...], hi[cols], CONTRACT_LANES, preferred_element_type=jnp.float32)
        small = lax.dot_general(own[:padded], lo[cols], CONTRACT_LANES, preferred_element_type=jnp.float32)
        gram = ((both[:padded] + both[padded:] + small) * (1.0 / snaps))[:rows]
        if n < tiles - 1:
            penalty = pen_ref[0:1, cols]
        else:
            rbuf[...] = gram[:, 128:256].T[:R]
            gram, row, col = gram[:, :128], row[:, :128], col[:, :128]
            penalty = jnp.concatenate([pen_ref[0:1, n * 256 : F], jnp.zeros((1, RATE_ROW - F), jnp.float32)], axis=1)
        gram = gram + jnp.where(row == col + n * 256, penalty, 0.0)
        if n < tiles - 1:
            obuf[:, cols] = gram
        else:
            cols = slice(n * 256, F)
            obuf[:, cols] = gram[:, : F - n * 256]
        copies.append(pltpu.make_async_copy(obuf.at[:, cols], normal_ref.at[:, cols], sem.at[n]))
        copies[-1].start()
    copies.append(pltpu.make_async_copy(rbuf, rhs_ref, sem.at[tiles]))
    copies[-1].start()
    for copy in copies:
        copy.wait()


def shards(snapshots, pod_basis, penalty):
    group, dofs = snapshots.shape
    hbm = pl.BlockSpec(memory_space=pltpu.HBM)
    vmem = pl.BlockSpec(memory_space=pltpu.VMEM)
    modes = pl.pallas_call(
        project_and_share,
        out_shape=jax.ShapeDtypeStruct((NT // 2, R, 128), jnp.float32),
        in_specs=[hbm, hbm],
        out_specs=vmem,
        scratch_shapes=[
            pltpu.VMEM((group, dofs), jnp.bfloat16),
            pltpu.VMEM((R, dofs), jnp.bfloat16),
            pltpu.VMEM((NX, HALF, 128), jnp.float32),
            pltpu.VMEM((NZ, HALF, 128), jnp.float32),
            pltpu.VMEM((NT, HALF, 128), jnp.float32),
            pltpu.SemaphoreType.DMA((2, CHUNKS)),
            pltpu.SemaphoreType.DMA((3,)),
            pltpu.SemaphoreType.DMA((3,)),
        ],
        compiler_params=pltpu.CompilerParams(
            collective_id=0, has_side_effects=True, vmem_limit_bytes=56 << 20
        ),
        name="project_and_share",
    )(snapshots, pod_basis)
    own_rows = (F + 1) // NT
    padded = -(-own_rows // 16) * 16
    groups = NT // 2
    normal, rhs, state, rates = pl.pallas_call(
        normal_equations,
        out_shape=[
            jax.ShapeDtypeStruct((own_rows, F), jnp.float32),
            jax.ShapeDtypeStruct((R, own_rows), jnp.float32),
            jax.ShapeDtypeStruct((1, 2, R), jnp.float32),
            jax.ShapeDtypeStruct((1, 2, R), jnp.float32),
        ],
        in_specs=[vmem, vmem],
        out_specs=[hbm, hbm, vmem, vmem],
        scratch_shapes=[
            pltpu.VMEM((groups, 80, 128), jnp.float32),
            pltpu.VMEM((groups, 128, 128), jnp.float32),
            pltpu.VMEM((groups, ROWS, 128), jnp.float32),
            pltpu.VMEM((ROWS, groups * 128), jnp.bfloat16),
            pltpu.VMEM((ROWS, groups * 128), jnp.bfloat16),
            pltpu.VMEM((2 * padded, groups * 128), jnp.bfloat16),
            pltpu.VMEM((2, 128, 128), jnp.float32),
            pltpu.VMEM((own_rows, F), jnp.float32),
            pltpu.VMEM((R, own_rows), jnp.float32),
            pltpu.SemaphoreType.DMA((ROWS // 256 + 1,)),
        ],
        compiler_params=pltpu.CompilerParams(vmem_limit_bytes=32 << 20),
        name="normal_equations",
    )(modes, penalty[None, :])
    return normal, rhs.T, state, rates


def solution(mesh):
    return jax.shard_map(
        shards,
        mesh=mesh,
        in_specs=(P("tm", "space"), P(None, "space"), P()),
        out_specs=(P("tm", None), P("tm", None), P("tm", "space", None), P("tm", "space", None)),
        check_vma=False,
    )
```

time: 120 us -> 35.2 us (0.29)
  local copies, waits for them, and re-layouts: 41.5 us -> 1.62 us
  Pallas kernels: 0 us -> 32.8 us
  starting transfers between devices: 28.7 us -> 0 us
  waiting for transfers between devices: 27.9 us -> 0 us
  matrix products: 14.8 us -> 0 us
  other arithmetic: 5.36 us -> 0 us
    pallas_call x0 -> x2, Pallas kernels: none -> 32.8 us  [the longest x1 27 us: shards(): pl.pallas_call(project_and_share, out_shape=jax.ShapeDtypeStruct((NT // 2...]
    all_to_all x3 -> x0, waiting for transfers between devices: 26.8 us -> none  [the longest x2 17.6 us: sent_to_all(): return lax.all_to_all(copies, axis, split_axis=0, concat_axis=0, tiled=True)]
    all_to_all x3 -> x0, starting transfers between devices: 21.7 us -> none  [the longest x2 11.6 us: sent_to_all(): return lax.all_to_all(copies, axis, split_axis=0, concat_axis=0, tiled=True)]
    dot_general x3 -> x0, matrix products: 14.8 us -> none  [the longest x1 7.17 us: normal_block(): lax.dot_general(columns, feature_all, dims, precision=lax.Precision.HIGHE...]
    concatenate x1 -> x0, local copies, waits for them, and re-layouts: 14.8 us -> none  [features(): return jnp.concatenate([constant, reduced, quadratic], axis=1)]
    gather x1 -> x0, local copies, waits for them, and re-layouts: 12.3 us -> none  [features(): quadratic = jnp.take(outer_prod, flat_index, axis=1)]
    mul x1 -> x0, local copies, waits for them, and re-layouts: 10.6 us -> none  [features(): reduced[:, :, None] * reduced[:, None, :]]
    ppermute x2 -> x0, starting transfers between devices: 7.07 us -> none  [the longest x1 5.15 us: padded_2(): lax.ppermute(lax.slice_in_dim(block, 0, width, axis=dim), axis, backward)]
  transfers between devices with their start and end apart: 5 -> 0, of which waited for: 4 -> 0; matrix products, arithmetic and copies ran while one was open for 1% -> 0% of each run, Pallas kernels for 0% -> 0%
where the time goes in v1:
time: 35.2 us; the launch traced here: 35.1 us
  Pallas kernels  32.8 us (93%)
  local copies, waits for them, and re-layouts  1.62 us (5%)
  between operations  0.65 us (2%)
    pallas_call x1, Pallas kernels, shards(): pl.pallas_call(project_and_share, out_shape=jax.ShapeDtypeStruct((NT // 2...  27 us
    pallas_call x1, Pallas kernels, shards(): pl.pallas_call(normal_equations, out_shape=[jax.ShapeDtypeStruct((own_row...  5.83 us
    unnamed x2, local copies, waits for them, and re-layouts  0.9 us
    broadcast_in_dim x1, local copies, waits for them, and re-layouts, shards(): penalty[None, :]  0.72 us

profile of v1, /device:TPU:1, one launch (start us, length us, event | category | flops | bytes accessed | tf_op | source)
XLA Modules:
  0.0 35.1 jit_solution(10889945420530699944)
XLA Ops:
  0.6 0.7 %broadcast_in_dim.3.pen_ref = f32[1,2415]{1,0:T(1,128)S(1)} reshape(f32[2415]{0:T(1024)} %param.5) | data formatting | bytes 19320 | tf_op jit(solution)/shard_map/broadcast_in_dim | solution.py:235
  1.3 27.0 %project_and_share.1.modes_ref = f32[4,68,128]{2,1,0:T(8,128)} custom-call(bf16[64,32768]{1,0:T(8,128)(2,1)} %snap_hbm.1, bf16[68,32768]{1,0:T(8,128)(2,1)} %pod_hbm.1), custom_call_target="tpu_custom_call" | custom-call | tf_op jit(solution)/shard_map/project_and_share/pallas_call | solution.py:188
  28.3 0.0 copy-start
  28.3 0.9 %copy-done = f32[4,68,128]{2,1,0:T(8,128)S(1)} copy-done((f32[4,68,128]{2,1,0:T(8,128)S(1)}, f32[4,68,128]{2,1,0:T(8,128)}, u32[]{:S(2)}) %copy-start) | copy-done | bytes 139288
  29.2 5.8 %normal_equations.1 = (f32[302,2415]{1,0:T(8,128)}, f32[68,302]{1,0:T(8,128)}, f32[1,2,68]{2,1,0:T(2,128)}, f32[1,2,68]{2,1,0:T(2,128)}) custom-call(f32[4,68,128]{2,1,0:T(8,128)S(1)} %copy-done, f32[1,2415]{1,0:T(1,128)S(1)} %broadcast_in_dim.3.pen_ref), custom_call_target="tpu_custom_call" | custom-call | tf_op jit(solution)/shard_map/normal_equations/pallas_call | solution.py:211
Async XLA Ops:
  28.3 0.9 %copy-start = (f32[4,68,128]{2,1,0:T(8,128)S(1)}, f32[4,68,128]{2,1,0:T(8,128)}, u32[]{:S(2)}) copy-start(f32[4,68,128]{2,1,0:T(8,128)} %project_and_share.1.modes_ref) | copy-start | bytes 417796

commit v2 on v1

v2 whole, which is shorter than its diff:
```python
import functools

import jax
import jax.numpy as jnp
from jax import lax
from jax.experimental import pallas as pl
from jax.experimental.pallas import tpu as pltpu
from jax.sharding import PartitionSpec as P

R = 68
HALF = R // 2
F = 1 + R + R * (R + 1) // 2
ROWS = 2560
RATE_ROW = 2432
EARLY = 2304
OWN = (F + 1) // 8
PAD = -(-OWN // 16) * 16
GROUPS = 4
NX, NZ, NT = 4, 8, 8
CHUNKS = 8
MESH = pl.DeviceIdType.MESH
CONTRACT_LANES = (((1,), (1,)), ((), ()))


def quadratic_rows():
    starts, at = [], 1 + R
    for i in range(R):
        starts.append(at)
        at += R - i
    return starts


def split(value):
    high = value.astype(jnp.bfloat16)
    return high, (value - high.astype(jnp.float32)).astype(jnp.bfloat16)


def products(own, hi, lo):
    both = lax.dot_general(own, hi, CONTRACT_LANES, preferred_element_type=jnp.float32)
    small = lax.dot_general(own[:PAD], lo, CONTRACT_LANES, preferred_element_type=jnp.float32)
    return both[:PAD] + both[PAD:] + small


def project_and_share(
    snap_hbm, pod_hbm, part_ref, own_ref, hi_ref, lo_ref, mine_ref,
    snap, pod, xbuf, zbuf, tbuf, modes, feat, turned, load_sem, send_sem, recv_sem
):
    space, tm = lax.axis_index("space"), lax.axis_index("tm")
    z, x = space // NX, lax.rem(space, NX)
    y, core = tm // 2, lax.rem(tm, 2)
    x_peers = [(z * NX + lax.rem(x + k, NX), tm) for k in range(1, NX)]
    z_peers = [(lax.rem(z + k, NZ) * NX + x, tm) for k in range(1, NZ)]
    chips = [lax.rem(y + k, GROUPS) for k in range(GROUPS)]
    sibling = (space, 2 * y + (1 - core))
    t_peers = [sibling] + [(space, 2 * chips[k] + c) for k in range(1, GROUPS) for c in range(2)]

    width = snap_hbm.shape[1] // CHUNKS

    def loads(i):
        cols = pl.ds(i * width, width)
        return (
            pltpu.make_async_copy(snap_hbm.at[:, cols], snap.at[:, cols], load_sem.at[0, i]),
            pltpu.make_async_copy(pod_hbm.at[:, cols], pod.at[:, cols], load_sem.at[1, i]),
        )

    for i in range(CHUNKS):
        for copy in loads(i):
            copy.start()

    barrier = pltpu.get_barrier_semaphore()
    peers = z_peers + t_peers + x_peers
    for peer in peers:
        pl.semaphore_signal(barrier, inc=1, device_id=peer, device_id_type=MESH)

    feat[:, 0:1] = jnp.ones((GROUPS, 1, 128), jnp.float32)
    modes[:, R:80] = jnp.zeros((GROUPS, 80 - R, 128), jnp.float32)

    total = jnp.zeros((R, snap_hbm.shape[0]), jnp.float32)
    for i in range(CHUNKS):
        for copy in loads(i):
            copy.wait()
        cols = slice(i * width, (i + 1) * width)
        total = total + lax.dot_general(
            pod[:, cols], snap[:, cols], CONTRACT_LANES, preferred_element_type=jnp.float32
        )
    packed = jnp.concatenate([total[:HALF], total[HALF:]], axis=1)

    pl.semaphore_wait(barrier, len(peers))

    def send(buf, rank, peer, phase):
        pltpu.make_async_remote_copy(
            src_ref=buf.at[rank],
            dst_ref=buf.at[rank],
            send_sem=send_sem.at[min(phase, 2)],
            recv_sem=recv_sem.at[phase],
            device_id=peer,
            device_id_type=MESH,
        ).start()

    def arrived(buf, at, count, sem):
        slots = buf.at[pl.ds(at, count)]
        pltpu.make_async_copy(slots, slots, sem).wait()

    xbuf[x] = packed
    for peer in x_peers:
        send(xbuf, x, peer, 0)
    arrived(xbuf, 0, NX - 1, recv_sem.at[0])
    zbuf[z] = (xbuf[0] + xbuf[1]) + (xbuf[2] + xbuf[3])
    for peer in z_peers:
        send(zbuf, z, peer, 1)
    arrived(zbuf, 0, NZ - 1, recv_sem.at[1])
    tbuf[tm] = ((zbuf[0] + zbuf[1]) + (zbuf[2] + zbuf[3])) + (
        (zbuf[4] + zbuf[5]) + (zbuf[6] + zbuf[7])
    )
    send(tbuf, tm, sibling, 2)
    for k in range(1, GROUPS):
        for c in range(2):
            send(tbuf, tm, (space, 2 * chips[GROUPS - k] + c), 2 + k)

    half_lane = lax.broadcasted_iota(jnp.int32, (HALF, 128), 1) < 64
    first_row = tm * OWN

    def build(k, count):
        for g in range(k, k + count):
            a, b = tbuf[2 * chips[g]], tbuf[2 * chips[g] + 1]
            modes[g, 0:HALF] = jnp.where(half_lane, a, pltpu.roll(b, 64, 1))
            modes[g, HALF:R] = jnp.where(half_lane, pltpu.roll(a, 64, 1), b)
        part = slice(k, k + count)
        feat[part, 1 : 1 + R] = modes[part, :R]
        for i, at in enumerate(quadratic_rows()):
            rows = -(-(R - i) // 8) * 8
            feat[part, at : at + rows] = modes[part, i : i + rows] * modes[part, i : i + 1]
        feat[part, F:RATE_ROW] = jnp.zeros((count, RATE_ROW - F, 128), jnp.float32)
        for g in range(k, k + count):
            lanes = slice(g * 128, (g + 1) * 128)
            own_ref[0:PAD, lanes], own_ref[PAD : 2 * PAD, lanes] = split(feat[g, pl.ds(first_row, PAD)])

            def step(r, carry, g=g, lanes=lanes):
                at = pl.ds(pl.multiple_of(r * 64, 64), 64)
                hi_ref[at, lanes], lo_ref[at, lanes] = split(feat[g, at])
                return carry

            lax.fori_loop(0, RATE_ROW // 64, step, 0, unroll=4)

    arrived(tbuf, sibling[1], 1, recv_sem.at[2])
    build(0, 1)
    arrived(tbuf, 2 * chips[1], 2, recv_sem.at[3])
    build(1, 1)
    for n in range(EARLY // 256):
        cols = slice(n * 256, (n + 1) * 256)
        part_ref[:, cols] = products(own_ref[:, :256], hi_ref[cols, :256], lo_ref[cols, :256])
    arrived(tbuf, 2 * chips[2], 2, recv_sem.at[4])
    arrived(tbuf, 2 * chips[3], 2, recv_sem.at[5])
    build(2, 2)

    snaps = GROUPS * 128
    whole = jnp.concatenate([modes[g, :72] for g in range(GROUPS)], axis=1)
    when = lax.rem(lax.broadcasted_iota(jnp.int32, (72, snaps), 1) + y * 128, snaps)
    first, last = when == 0, when == snaps - 1
    after = jnp.where(last, whole, pltpu.roll(whole, snaps - 1, 1))
    before = jnp.where(first, whole, pltpu.roll(whole, 1, 1))
    rate = (after - before) * jnp.where(first | last, 1.0, 0.5)
    rate = jnp.concatenate([rate, jnp.zeros((ROWS - RATE_ROW - 72, snaps), jnp.float32)], axis=0)
    hi_ref[RATE_ROW:ROWS], lo_ref[RATE_ROW:ROWS] = split(rate)

    at = core * 64 + 2 * space
    turned[0] = jnp.concatenate([modes[0], jnp.zeros((48, 128), jnp.float32)], axis=0).T
    turned[1] = rate[:, :128].T
    mine_ref[0] = turned[0, pl.ds(at, 2)]
    mine_ref[1] = turned[1, pl.ds(at, 2)]

    for phase, (buf, count) in enumerate(((xbuf, NX - 1), (zbuf, NZ - 1), (tbuf, NT - 1))):
        arrived(buf, 0, count, send_sem.at[phase])


def normal_equations(
    part_ref, own_ref, hi_ref, lo_ref, mine_ref, pen_ref, normal_ref, rhs_ref, state_ref, rate_ref, obuf, rbuf, sem
):
    first_row = lax.axis_index("tm") * OWN
    state_ref[0] = mine_ref[0, :, :R]
    rate_ref[0] = mine_ref[1, :, :R]
    row = lax.broadcasted_iota(jnp.int32, (OWN, 256), 0) + first_row
    col = lax.broadcasted_iota(jnp.int32, (OWN, 256), 1)
    scale = 1.0 / (GROUPS * 128)
    copies = []
    for n in range(ROWS // 256):
        at = slice(n * 256, (n + 1) * 256)
        if n * 256 < EARLY:
            cols, late = at, slice(256, 512)
            gram = products(own_ref[:, late], hi_ref[at, late], lo_ref[at, late]) + part_ref[:, at]
        else:
            cols = slice(n * 256, F)
            gram = products(own_ref[...], hi_ref[at], lo_ref[at])
            rbuf[...] = (gram[:OWN, 128:256] * scale).T[:R]
            gram, row, col = gram[:, : F - n * 256], row[:, : F - n * 256], col[:, : F - n * 256]
        penalty = pen_ref[cols][None, :]
        obuf[:, cols] = gram[:OWN] * scale + jnp.where(row == col + n * 256, penalty, 0.0)
        copies.append(pltpu.make_async_copy(obuf.at[:, cols], normal_ref.at[:, cols], sem.at[n]))
        copies[-1].start()
    copies.append(pltpu.make_async_copy(rbuf, rhs_ref, sem.at[ROWS // 256]))
    copies[-1].start()
    for copy in copies:
        copy.wait()


def shards(snapshots, pod_basis, penalty):
    group, dofs = snapshots.shape
    snaps = GROUPS * 128
    hbm = pl.BlockSpec(memory_space=pltpu.HBM)
    vmem = pl.BlockSpec(memory_space=pltpu.VMEM)
    shared = pl.pallas_call(
        project_and_share,
        out_shape=[
            pltpu.VMEM((PAD, EARLY), jnp.float32),
            pltpu.VMEM((2 * PAD, snaps), jnp.bfloat16),
            pltpu.VMEM((ROWS, snaps), jnp.bfloat16),
            pltpu.VMEM((ROWS, snaps), jnp.bfloat16),
            pltpu.VMEM((2, 2, 128), jnp.float32),
        ],
        in_specs=[hbm, hbm],
        out_specs=[vmem] * 5,
        scratch_shapes=[
            pltpu.VMEM((group, dofs), jnp.bfloat16),
            pltpu.VMEM((R, dofs), jnp.bfloat16),
            pltpu.VMEM((NX, HALF, 128), jnp.float32),
            pltpu.VMEM((NZ, HALF, 128), jnp.float32),
            pltpu.VMEM((NT, HALF, 128), jnp.float32),
            pltpu.VMEM((GROUPS, 80, 128), jnp.float32),
            pltpu.VMEM((GROUPS, RATE_ROW + 16, 128), jnp.float32),
            pltpu.VMEM((2, 128, 128), jnp.float32),
            pltpu.SemaphoreType.DMA((2, CHUNKS)),
            pltpu.SemaphoreType.DMA((3,)),
            pltpu.SemaphoreType.DMA((6,)),
        ],
        compiler_params=pltpu.CompilerParams(
            collective_id=0, has_side_effects=True, vmem_limit_bytes=50 << 20
        ),
        name="project_and_share",
    )(snapshots, pod_basis)
    normal, rhs, state, rates = pl.pallas_call(
        normal_equations,
        out_shape=[
            jax.ShapeDtypeStruct((OWN, F), jnp.float32),
            jax.ShapeDtypeStruct((R, OWN), jnp.float32),
            jax.ShapeDtypeStruct((1, 2, R), jnp.float32),
            jax.ShapeDtypeStruct((1, 2, R), jnp.float32),
        ],
        in_specs=[vmem] * 6,
        out_specs=[hbm, hbm, vmem, vmem],
        scratch_shapes=[
            pltpu.VMEM((OWN, F), jnp.float32),
            pltpu.VMEM((R, OWN), jnp.float32),
            pltpu.SemaphoreType.DMA((ROWS // 256 + 1,)),
        ],
        compiler_params=pltpu.CompilerParams(vmem_limit_bytes=16 << 20),
        name="normal_equations",
    )(*shared, penalty)
    return normal, rhs.T, state, rates


def solution(mesh):
    return jax.shard_map(
        shards,
        mesh=mesh,
        in_specs=(P("tm", "space"), P(None, "space"), P()),
        out_specs=(P("tm", None), P("tm", None), P("tm", "space", None), P("tm", "space", None)),
        check_vma=False,
    )
```

time: 35.2 us -> 32 us (0.909)
  local copies, waits for them, and re-layouts: 1.62 us -> 0.01 us
  Pallas kernels: 32.8 us -> 31.2 us
    pallas_call x2, Pallas kernels: 32.8 us -> 31.2 us  [the longest x1 28.1 us: shards(): pl.pallas_call(project_and_share, out_shape=[pltpu.VMEM((PAD, EARLY), jnp...]
    unnamed x2, local copies, waits for them, and re-layouts: 0.9 us -> 0.01 us
    broadcast_in_dim x1 -> x0, local copies, waits for them, and re-layouts: 0.72 us -> none  [shards(): penalty[None, :]]
where the time goes in v2:
time: 32 us; the launch traced here: 31.9 us
  Pallas kernels  31.2 us (98%)
  between operations  0.65 us (2%)
    pallas_call x1, Pallas kernels, shards(): pl.pallas_call(project_and_share, out_shape=[pltpu.VMEM((PAD, EARLY), jnp...  28.1 us
    pallas_call x1, Pallas kernels, shards(): pl.pallas_call(normal_equations, out_shape=[jax.ShapeDtypeStruct((OWN, F)...  3.12 us

profile of v2, /device:TPU:1, one launch (start us, length us, event | category | flops | bytes accessed | tf_op | source)
XLA Modules:
  0.0 31.9 jit_solution(3321504636981468962)
XLA Ops:
  0.6 0.0 copy-start
  0.6 28.1 %project_and_share.1 = (f32[304,2304]{1,0:T(8,128)S(1)}, bf16[608,512]{1,0:T(8,128)(2,1)S(1)}, bf16[2560,512]{1,0:T(8,128)(2,1)S(1)}, bf16[2560,512]{1,0:T(8,128)(2,1)S(1)}, f32[2,2,128]{2,1,0:T(2,128)S(1)}) custom-call(bf16[64,32768]{1,0:T(8,128)(2,1)} %snap_hbm.1, bf16[68,32768]{1,0:T(8,128)(2,1)} %pod_hbm.1), custom_call_target="tpu_custom_call" | custom-call | tf_op jit(solution)/shard_map/project_and_share/pallas_call | solution.py:211
  28.8 0.0 copy-done
  28.8 3.1 %normal_equations.1 = (f32[302,2415]{1,0:T(8,128)}, f32[68,302]{1,0:T(8,128)}, f32[1,2,68]{2,1,0:T(2,128)}, f32[1,2,68]{2,1,0:T(2,128)}) custom-call(f32[304,2304]{1,0:T(8,128)S(1)} %get-tuple-element.13.part_ref, bf16[608,512]{1,0:T(8,128)(2,1)S(1)} %get-tuple-element.14.own_ref, bf16[2560,512]{1,0:T(8,128)(2,1)S(1)} %get-tuple-element.15.hi_ref, ...), custom_call_target="tpu_custom_call" | custom-call | tf_op jit(solution)/shard_map/normal_equations/pallas_call | solution.py:240
Async XLA Ops:
  0.6 28.1 %copy-start = (f32[2415]{0:T(1024)S(1)}, f32[2415]{0:T(1024)}, u32[]{:S(2)}) copy-start(f32[2415]{0:T(1024)} %pen_ref.1) | copy-start | bytes 28984

commit v3 on v2

v3 whole, which is shorter than its diff:
```python
import functools

import jax
import jax.numpy as jnp
from jax import lax
from jax.experimental import pallas as pl
from jax.experimental.pallas import tpu as pltpu
from jax.sharding import PartitionSpec as P

R = 68
HALF = R // 2
F = 1 + R + R * (R + 1) // 2
OWN = (F + 1) // 8
PAD = -(-OWN // 16) * 16
GROUPS = 4
NX, NZ, NT = 4, 8, 8
CHUNKS = (2048, 6144, 6144, 6144, 4096, 4096, 2048, 1024, 1024)
SLOTS = (0, 1, 3, 2)
LAST = 2432
MESH = pl.DeviceIdType.MESH
CONTRACT_LANES = (((1,), (1,)), ((), ()))


def quadratic_rows():
    starts, at = [], 1 + R
    for i in range(R):
        starts.append(at)
        at += R - i
    return starts


def split(value):
    high = value.astype(jnp.bfloat16)
    return high, (value - high.astype(jnp.float32)).astype(jnp.bfloat16)


def dot(a, b):
    return lax.dot_general(a, b, CONTRACT_LANES, preferred_element_type=jnp.float32)


def tiles():
    return [(at, min(at + 256, LAST)) for at in range(0, LAST, 256)]


def pair_products(own, hi, lo):
    both = dot(own, hi)
    return both[:PAD] + both[PAD:] + dot(own[:PAD], lo)


def single_products(own, hi, lo):
    high = own[:PAD]
    whole = dot(jnp.concatenate([high, high], axis=1), jnp.concatenate([hi, lo], axis=1))
    return whole + dot(own[PAD:], hi)


def project_and_share(
    snap_hbm, pod_hbm, part_ref, own_ref, late_ref, modes,
    snap, pod, xbuf, zbuf, tbuf, feat, load_sem, send_sem, recv_sem
):
    space, tm = lax.axis_index("space"), lax.axis_index("tm")
    z, x = space // NX, lax.rem(space, NX)
    y, core = tm // 2, lax.rem(tm, 2)
    x_peers = [(z * NX + lax.rem(x + k, NX), tm) for k in (2, 1, 3)]
    z_peers = [(lax.rem(z + k, NZ) * NX + x, tm) for k in (4, 3, 5, 2, 6, 1, 7)]
    chips = [lax.rem(y + k, GROUPS) for k in range(GROUPS)]
    sibling = (space, 2 * y + (1 - core))
    t_peers = [sibling] + [(space, 2 * chips[k] + c) for k in range(1, GROUPS) for c in range(2)]

    loads, at = [], 0
    for i, width in enumerate(CHUNKS):
        cols = slice(at, at + width)
        at += width
        loads.append((
            cols,
            pltpu.make_async_copy(snap_hbm.at[:, cols], snap.at[:, cols], load_sem.at[0, i]),
            pltpu.make_async_copy(pod_hbm.at[:, cols], pod.at[:, cols], load_sem.at[1, i]),
        ))
    for _, first, second in loads:
        first.start()
        second.start()

    barrier = pltpu.get_barrier_semaphore()
    peers = z_peers + t_peers + x_peers
    for peer in peers:
        pl.semaphore_signal(barrier, inc=1, device_id=peer, device_id_type=MESH)

    for g in range(GROUPS):
        place(feat, late_ref, g, slice(0, 1), jnp.ones((1, 128), jnp.float32))
    modes[:, R:80] = jnp.zeros((GROUPS, 80 - R, 128), jnp.float32)

    total = jnp.zeros((R, snap_hbm.shape[0]), jnp.float32)
    for cols, first, second in loads:
        first.wait()
        second.wait()
        total = total + dot(pod[:, cols], snap[:, cols])
    packed = jnp.concatenate([total[:HALF], total[HALF:]], axis=1)

    pl.semaphore_wait(barrier, len(peers))

    def send(buf, rank, peer, phase):
        pltpu.make_async_remote_copy(
            src_ref=buf.at[rank],
            dst_ref=buf.at[rank],
            send_sem=send_sem.at[min(phase, 2)],
            recv_sem=recv_sem.at[phase],
            device_id=peer,
            device_id_type=MESH,
        ).start()

    def arrived(buf, at, count, sem):
        slots = buf.at[pl.ds(at, count)]
        pltpu.make_async_copy(slots, slots, sem).wait()

    xbuf[x] = packed
    for peer in x_peers:
        send(xbuf, x, peer, 0)
    arrived(xbuf, 0, NX - 1, recv_sem.at[0])
    zbuf[z] = (xbuf[0] + xbuf[1]) + (xbuf[2] + xbuf[3])
    for peer in z_peers:
        send(zbuf, z, peer, 1)
    arrived(zbuf, 0, NZ - 1, recv_sem.at[1])
    tbuf[tm] = ((zbuf[0] + zbuf[1]) + (zbuf[2] + zbuf[3])) + (
        (zbuf[4] + zbuf[5]) + (zbuf[6] + zbuf[7])
    )
    send(tbuf, tm, sibling, 2)
    for k in SLOTS[1:]:
        for c in range(2):
            send(tbuf, tm, (space, 2 * chips[GROUPS - k] + c), 2 + k)

    half_lane = lax.broadcasted_iota(jnp.int32, (HALF, 128), 1) < 64
    first_row = tm * OWN

    def build(g):
        chip = chips[SLOTS[g]]
        a, b = tbuf[2 * chip], tbuf[2 * chip + 1]
        modes[g, 0:HALF] = jnp.where(half_lane, a, pltpu.roll(b, 64, 1))
        modes[g, HALF:R] = jnp.where(half_lane, pltpu.roll(a, 64, 1), b)
        place(feat, late_ref, g, slice(1, 1 + R), modes[g, :R])
        for i, at in enumerate(quadratic_rows()):
            rows = -(-(R - i) // 8) * 8
            place(feat, late_ref, g, slice(at, at + rows), modes[g, i : i + rows] * modes[g, i : i + 1])
        place(feat, late_ref, g, slice(F, LAST), jnp.zeros((LAST - F, 128), jnp.float32))
        mine = pl.ds(first_row, PAD)
        value = late_ref[mine] if g == GROUPS - 1 else feat[g, mine]
        lanes = slice(g * 128, (g + 1) * 128)
        own_ref[0:PAD, lanes], own_ref[PAD : 2 * PAD, lanes] = split(value)

    arrived(tbuf, sibling[1], 1, recv_sem.at[2])
    build(0)
    own = own_ref[:, 0:128]
    for at, end in tiles():
        part_ref[:, at:end] = single_products(own, *split(feat[0, at:end]))
    arrived(tbuf, 2 * chips[1], 2, recv_sem.at[3])
    build(1)
    arrived(tbuf, 2 * chips[3], 2, recv_sem.at[5])
    build(2)
    own = own_ref[:, 128:384]
    for at, end in tiles():
        value = jnp.concatenate([feat[1, at:end], feat[2, at:end]], axis=1)
        part_ref[:, at:end] += pair_products(own, *split(value))
    arrived(tbuf, 2 * chips[2], 2, recv_sem.at[4])
    build(3)

    for phase, (buf, count) in enumerate(((xbuf, NX - 1), (zbuf, NZ - 1), (tbuf, NT - 1))):
        arrived(buf, 0, count, send_sem.at[phase])


def place(feat, late_ref, g, rows, value):
    if g == GROUPS - 1:
        late_ref[rows] = value
    else:
        feat[g, rows] = value


def normal_equations(
    part_ref, own_ref, late_ref, modes, pen_ref, normal_ref, rhs_ref, state_ref, rate_ref, turned, obuf, rbuf, sem
):
    space, tm = lax.axis_index("space"), lax.axis_index("tm")
    first_row = tm * OWN
    snaps = GROUPS * 128
    scale = 1.0 / snaps
    own = own_ref[:, (GROUPS - 1) * 128 :]
    copies = []
    for n, (at, end) in enumerate(tiles()):
        cols = slice(at, min(end, F))
        width = cols.stop - at
        gram = single_products(own, *split(late_ref[at:end])) + part_ref[:, at:end]
        row = lax.broadcasted_iota(jnp.int32, (OWN, width), 0) + first_row
        col = lax.broadcasted_iota(jnp.int32, (OWN, width), 1) + at
        obuf[:, cols] = gram[:OWN, :width] * scale + jnp.where(row == col, pen_ref[cols][None, :], 0.0)
        copies.append(pltpu.make_async_copy(obuf.at[:, cols], normal_ref.at[:, cols], sem.at[n]))
        copies[-1].start()

        if n == 2:
            order = [modes[SLOTS.index(k), :72] for k in range(GROUPS)]
            whole = jnp.concatenate(order, axis=1)
            when = lax.rem(lax.broadcasted_iota(jnp.int32, (72, snaps), 1) + (tm // 2) * 128, snaps)
            first, last = when == 0, when == snaps - 1
            after = jnp.where(last, whole, pltpu.roll(whole, snaps - 1, 1))
            before = jnp.where(first, whole, pltpu.roll(whole, 1, 1))
            rate = (after - before) * jnp.where(first | last, 1.0, 0.5)
            rate = jnp.concatenate([rate, jnp.zeros((56, snaps), jnp.float32)], axis=0)
            turned[0] = jnp.concatenate([whole[:, :128], jnp.zeros((56, 128), jnp.float32)], axis=0).T
            turned[1] = rate[:, :128].T
            mine = lax.rem(tm, 2) * 64 + 2 * space
            state_ref[0] = turned[0, pl.ds(mine, 2)][:, :R]
            rate_ref[0] = turned[1, pl.ds(mine, 2)][:, :R]
            rate = jnp.concatenate([rate[:, 128 * k : 128 * (k + 1)] for k in SLOTS], axis=1)
            rhs = pair_products(own_ref[...], *split(rate))
            rbuf[...] = (rhs[:OWN] * scale).T[:R]
            copies.append(pltpu.make_async_copy(rbuf, rhs_ref, sem.at[len(tiles())]))
            copies[-1].start()
    for copy in copies:
        copy.wait()


def shards(snapshots, pod_basis, penalty):
    group, dofs = snapshots.shape
    snaps = GROUPS * 128
    hbm = pl.BlockSpec(memory_space=pltpu.HBM)
    vmem = pl.BlockSpec(memory_space=pltpu.VMEM)
    shared = pl.pallas_call(
        project_and_share,
        out_shape=[
            pltpu.VMEM((PAD, LAST), jnp.float32),
            pltpu.VMEM((2 * PAD, snaps), jnp.bfloat16),
            pltpu.VMEM((LAST, 128), jnp.float32),
            pltpu.VMEM((GROUPS, 80, 128), jnp.float32),
        ],
        in_specs=[hbm, hbm],
        out_specs=[vmem] * 4,
        scratch_shapes=[
            pltpu.VMEM((group, dofs), jnp.bfloat16),
            pltpu.VMEM((R, dofs), jnp.bfloat16),
            pltpu.VMEM((NX, HALF, 128), jnp.float32),
            pltpu.VMEM((NZ, HALF, 128), jnp.float32),
            pltpu.VMEM((NT, HALF, 128), jnp.float32),
            pltpu.VMEM((GROUPS - 1, LAST, 128), jnp.float32),
            pltpu.SemaphoreType.DMA((2, len(CHUNKS))),
            pltpu.SemaphoreType.DMA((3,)),
            pltpu.SemaphoreType.DMA((6,)),
        ],
        compiler_params=pltpu.CompilerParams(
            collective_id=0, has_side_effects=True, vmem_limit_bytes=54 << 20
        ),
        name="project_and_share",
    )(snapshots, pod_basis)
    normal, rhs, state, rates = pl.pallas_call(
        normal_equations,
        out_shape=[
            jax.ShapeDtypeStruct((OWN, F), jnp.float32),
            jax.ShapeDtypeStruct((R, OWN), jnp.float32),
            jax.ShapeDtypeStruct((1, 2, R), jnp.float32),
            jax.ShapeDtypeStruct((1, 2, R), jnp.float32),
        ],
        in_specs=[vmem] * 5,
        out_specs=[hbm, hbm, vmem, vmem],
        scratch_shapes=[
            pltpu.VMEM((2, 128, 128), jnp.float32),
            pltpu.VMEM((OWN, F), jnp.float32),
            pltpu.VMEM((R, OWN), jnp.float32),
            pltpu.SemaphoreType.DMA((len(tiles()) + 1,)),
        ],
        compiler_params=pltpu.CompilerParams(vmem_limit_bytes=16 << 20),
        name="normal_equations",
    )(*shared, penalty)
    return normal, rhs.T, state, rates


def solution(mesh):
    return jax.shard_map(
        shards,
        mesh=mesh,
        in_specs=(P("tm", "space"), P(None, "space"), P()),
        out_specs=(P("tm", None), P("tm", None), P("tm", "space", None), P("tm", "space", None)),
        check_vma=False,
    )
```

time: 32 us -> 31.1 us (0.972)
  Pallas kernels: 31.2 us -> 30.3 us
    pallas_call x1, Pallas kernels: 28.1 us -> 27.4 us  [shards(): pl.pallas_call(project_and_share, out_shape=[pltpu.VMEM((PAD, LAST), jnp....]
where the time goes in v3:
time: 31.1 us; the launch traced here: 31 us
  Pallas kernels  30.3 us (97%)
  between operations  0.65 us (2%)
    pallas_call x1, Pallas kernels, shards(): pl.pallas_call(project_and_share, out_shape=[pltpu.VMEM((PAD, LAST), jnp....  27.4 us
    pallas_call x1, Pallas kernels, shards(): pl.pallas_call(normal_equations, out_shape=[jax.ShapeDtypeStruct((OWN, F)...  2.98 us

profile of v3, /device:TPU:1, one launch (start us, length us, event | category | flops | bytes accessed | tf_op | source)
XLA Modules:
  0.0 31.0 jit_solution(15384607095505350262)
XLA Ops:
  0.6 0.0 copy-start
  0.6 27.4 %project_and_share.1 = (f32[304,2432]{1,0:T(8,128)S(1)}, bf16[608,512]{1,0:T(8,128)(2,1)S(1)}, f32[2432,128]{1,0:T(8,128)S(1)}, f32[4,80,128]{2,1,0:T(8,128)S(1)}) custom-call(bf16[64,32768]{1,0:T(8,128)(2,1)} %snap_hbm.1, bf16[68,32768]{1,0:T(8,128)(2,1)} %pod_hbm.1), custom_call_target="tpu_custom_call" | custom-call | tf_op jit(solution)/shard_map/project_and_share/pallas_call | solution.py:222
  28.0 0.0 copy-done
  28.0 3.0 %normal_equations.1 = (f32[302,2415]{1,0:T(8,128)}, f32[68,302]{1,0:T(8,128)}, f32[1,2,68]{2,1,0:T(2,128)}, f32[1,2,68]{2,1,0:T(2,128)}) custom-call(f32[304,2432]{1,0:T(8,128)S(1)} %get-tuple-element.12.part_ref, bf16[608,512]{1,0:T(8,128)(2,1)S(1)} %get-tuple-element.13.own_ref, f32[2432,128]{1,0:T(8,128)S(1)} %get-tuple-element.14.late_ref, ...), custom_call_target="tpu_custom_call" | custom-call | tf_op jit(solution)/shard_map/normal_equations/pallas_call | solution.py:248
Async XLA Ops:
  0.6 27.4 %copy-start = (f32[2415]{0:T(1024)S(1)}, f32[2415]{0:T(1024)}, u32[]{:S(2)}) copy-start(f32[2415]{0:T(1024)} %pen_ref.1) | copy-start | bytes 28984

commit v4 on v3

--- a/solution.py
+++ b/solution.py
@@ -54,8 +54,8 @@
 
 
 def project_and_share(
-    snap_hbm, pod_hbm, part_ref, own_ref, late_ref, modes,
-    snap, pod, xbuf, zbuf, tbuf, feat, load_sem, send_sem, recv_sem
+    snap_hbm, pod_hbm, pen_hbm, part_ref, own_ref, late_ref, modes,
+    snap, pod, pen, xbuf, zbuf, tbuf, feat, load_sem, pen_sem, send_sem, recv_sem
 ):
     space, tm = lax.axis_index("space"), lax.axis_index("tm")
     z, x = space // NX, lax.rem(space, NX)
@@ -78,6 +78,8 @@
     for _, first, second in loads:
         first.start()
         second.start()
+    pen_copy = pltpu.make_async_copy(pen_hbm, pen, pen_sem)
+    pen_copy.start()
 
     barrier = pltpu.get_barrier_semaphore()
     peers = z_peers + t_peers + x_peers
@@ -141,23 +143,29 @@
             place(feat, late_ref, g, slice(at, at + rows), modes[g, i : i + rows] * modes[g, i : i + 1])
         place(feat, late_ref, g, slice(F, LAST), jnp.zeros((LAST - F, 128), jnp.float32))
         mine = pl.ds(first_row, PAD)
-        value = late_ref[mine] if g == GROUPS - 1 else feat[g, mine]
+        value = (feat[g, mine] if g < 2 else late_ref[g - 2, mine]) * (1.0 / (GROUPS * 128))
         lanes = slice(g * 128, (g + 1) * 128)
         own_ref[0:PAD, lanes], own_ref[PAD : 2 * PAD, lanes] = split(value)
 
     arrived(tbuf, sibling[1], 1, recv_sem.at[2])
     build(0)
+    pen_copy.wait()
     own = own_ref[:, 0:128]
     for at, end in tiles():
-        part_ref[:, at:end] = single_products(own, *split(feat[0, at:end]))
+        penalty = pen[at : min(end, F)][None, :]
+        if end > F:
+            penalty = jnp.concatenate([penalty, jnp.zeros((1, end - F), jnp.float32)], axis=1)
+        row = lax.broadcasted_iota(jnp.int32, (PAD, end - at), 0) + first_row
+        col = lax.broadcasted_iota(jnp.int32, (PAD, end - at), 1) + at
+        diagonal = jnp.where(row == col, penalty, 0.0)
+        part_ref[:, at:end] = single_products(own, *split(feat[0, at:end])) + diagonal
     arrived(tbuf, 2 * chips[1], 2, recv_sem.at[3])
     build(1)
+    own = own_ref[:, 128:256]
+    for at, end in tiles():
+        part_ref[:, at:end] += single_products(own, *split(feat[1, at:end]))
     arrived(tbuf, 2 * chips[3], 2, recv_sem.at[5])
     build(2)
-    own = own_ref[:, 128:384]
-    for at, end in tiles():
-        value = jnp.concatenate([feat[1, at:end], feat[2, at:end]], axis=1)
-        part_ref[:, at:end] += pair_products(own, *split(value))
     arrived(tbuf, 2 * chips[2], 2, recv_sem.at[4])
     build(3)
 
@@ -166,32 +174,32 @@
 
 
 def place(feat, late_ref, g, rows, value):
-    if g == GROUPS - 1:
-        late_ref[rows] = value
+    if g < 2:
+        feat[g, rows] = value
     else:
-        feat[g, rows] = value
+        late_ref[g - 2, rows] = value
 
 
 def normal_equations(
-    part_ref, own_ref, late_ref, modes, pen_ref, normal_ref, rhs_ref, state_ref, rate_ref, turned, obuf, rbuf, sem
+    part_ref, own_ref, late_ref, modes, normal_ref, rhs_ref, state_ref, rate_ref, turned, obuf, rbuf, mine, sem
 ):
     space, tm = lax.axis_index("space"), lax.axis_index("tm")
-    first_row = tm * OWN
     snaps = GROUPS * 128
-    scale = 1.0 / snaps
-    own = own_ref[:, (GROUPS - 1) * 128 :]
+    own = own_ref[:, snaps // 2 :]
     copies = []
+
+    def write(source, target, n):
+        copies.append(pltpu.make_async_copy(source, target, sem.at[n]))
+        copies[-1].start()
+
     for n, (at, end) in enumerate(tiles()):
         cols = slice(at, min(end, F))
-        width = cols.stop - at
-        gram = single_products(own, *split(late_ref[at:end])) + part_ref[:, at:end]
-        row = lax.broadcasted_iota(jnp.int32, (OWN, width), 0) + first_row
-        col = lax.broadcasted_iota(jnp.int32, (OWN, width), 1) + at
-        obuf[:, cols] = gram[:OWN, :width] * scale + jnp.where(row == col, pen_ref[cols][None, :], 0.0)
-        copies.append(pltpu.make_async_copy(obuf.at[:, cols], normal_ref.at[:, cols], sem.at[n]))
-        copies[-1].start()
-
-        if n == 2:
+        value = jnp.concatenate([late_ref[0, at:end], late_ref[1, at:end]], axis=1)
+        gram = pair_products(own, *split(value)) + part_ref[:, at:end]
+        obuf[:, cols] = gram[:OWN, : cols.stop - at]
+        write(obuf.at[:, cols], normal_ref.at[:, cols], n)
+
+        if n == 6:
             order = [modes[SLOTS.index(k), :72] for k in range(GROUPS)]
             whole = jnp.concatenate(order, axis=1)
             when = lax.rem(lax.broadcasted_iota(jnp.int32, (72, snaps), 1) + (tm // 2) * 128, snaps)
@@ -202,14 +210,15 @@
             rate = jnp.concatenate([rate, jnp.zeros((56, snaps), jnp.float32)], axis=0)
             turned[0] = jnp.concatenate([whole[:, :128], jnp.zeros((56, 128), jnp.float32)], axis=0).T
             turned[1] = rate[:, :128].T
-            mine = lax.rem(tm, 2) * 64 + 2 * space
-            state_ref[0] = turned[0, pl.ds(mine, 2)][:, :R]
-            rate_ref[0] = turned[1, pl.ds(mine, 2)][:, :R]
+            here = lax.rem(tm, 2) * 64 + 2 * space
+            mine[0, 0] = turned[0, pl.ds(here, 2)][:, :R]
+            mine[1, 0] = turned[1, pl.ds(here, 2)][:, :R]
+            write(mine.at[0], state_ref, len(tiles()) + 1)
+            write(mine.at[1], rate_ref, len(tiles()) + 2)
             rate = jnp.concatenate([rate[:, 128 * k : 128 * (k + 1)] for k in SLOTS], axis=1)
             rhs = pair_products(own_ref[...], *split(rate))
-            rbuf[...] = (rhs[:OWN] * scale).T[:R]
-            copies.append(pltpu.make_async_copy(rbuf, rhs_ref, sem.at[len(tiles())]))
-            copies[-1].start()
+            rbuf[...] = rhs[:OWN].T[:R]
+            write(rbuf, rhs_ref, len(tiles()))
     for copy in copies:
         copy.wait()
 
@@ -224,27 +233,29 @@
         out_shape=[
             pltpu.VMEM((PAD, LAST), jnp.float32),
             pltpu.VMEM((2 * PAD, snaps), jnp.bfloat16),
-            pltpu.VMEM((LAST, 128), jnp.float32),
+            pltpu.VMEM((2, LAST, 128), jnp.float32),
             pltpu.VMEM((GROUPS, 80, 128), jnp.float32),
         ],
-        in_specs=[hbm, hbm],
+        in_specs=[hbm, hbm, hbm],
         out_specs=[vmem] * 4,
         scratch_shapes=[
             pltpu.VMEM((group, dofs), jnp.bfloat16),
             pltpu.VMEM((R, dofs), jnp.bfloat16),
+            pltpu.VMEM((F,), jnp.float32),
             pltpu.VMEM((NX, HALF, 128), jnp.float32),
             pltpu.VMEM((NZ, HALF, 128), jnp.float32),
             pltpu.VMEM((NT, HALF, 128), jnp.float32),
-            pltpu.VMEM((GROUPS - 1, LAST, 128), jnp.float32),
+            pltpu.VMEM((2, LAST, 128), jnp.float32),
             pltpu.SemaphoreType.DMA((2, len(CHUNKS))),
+            pltpu.SemaphoreType.DMA,
             pltpu.SemaphoreType.DMA((3,)),
             pltpu.SemaphoreType.DMA((6,)),
         ],
         compiler_params=pltpu.CompilerParams(
-            collective_id=0, has_side_effects=True, vmem_limit_bytes=54 << 20
+            collective_id=0, has_side_effects=True, vmem_limit_bytes=53 << 20
         ),
         name="project_and_share",
-    )(snapshots, pod_basis)
+    )(snapshots, pod_basis, penalty)
     normal, rhs, state, rates = pl.pallas_call(
         normal_equations,
         out_shape=[
@@ -253,17 +264,18 @@
             jax.ShapeDtypeStruct((1, 2, R), jnp.float32),
             jax.ShapeDtypeStruct((1, 2, R), jnp.float32),
         ],
-        in_specs=[vmem] * 5,
-        out_specs=[hbm, hbm, vmem, vmem],
+        in_specs=[vmem] * 4,
+        out_specs=[hbm] * 4,
         scratch_shapes=[
             pltpu.VMEM((2, 128, 128), jnp.float32),
             pltpu.VMEM((OWN, F), jnp.float32),
             pltpu.VMEM((R, OWN), jnp.float32),
-            pltpu.SemaphoreType.DMA((len(tiles()) + 1,)),
+            pltpu.VMEM((2, 1, 2, R), jnp.float32),
+            pltpu.SemaphoreType.DMA((len(tiles()) + 3,)),
         ],
         compiler_params=pltpu.CompilerParams(vmem_limit_bytes=16 << 20),
         name="normal_equations",
-    )(*shared, penalty)
+    )(*shared)
     return normal, rhs.T, state, rates
 
 

time: 31.1 us -> 29.1 us (0.936)
  Pallas kernels: 30.3 us -> 28.4 us
    pallas_call x1, Pallas kernels: 27.4 us -> 25.7 us  [shards(): pl.pallas_call(project_and_share, out_shape=[pltpu.VMEM((PAD, LAST), jnp....]
    pallas_call x1, Pallas kernels: 2.98 us -> 2.66 us  [shards(): pl.pallas_call(normal_equations, out_shape=[jax.ShapeDtypeStruct((OWN, F)...]
where the time goes in v4:
time: 29.1 us; the launch traced here: 29 us
  Pallas kernels  28.4 us (98%)
  between operations  0.64 us (2%)
    pallas_call x1, Pallas kernels, shards(): pl.pallas_call(project_and_share, out_shape=[pltpu.VMEM((PAD, LAST), jnp....  25.7 us
    pallas_call x1, Pallas kernels, shards(): pl.pallas_call(normal_equations, out_shape=[jax.ShapeDtypeStruct((OWN, F)...  2.66 us

profile of v4, /device:TPU:1, one launch (start us, length us, event | category | flops | bytes accessed | tf_op | source)
XLA Modules:
  0.0 29.0 jit_solution(17910879903296736884)
XLA Ops:
  0.6 25.7 %project_and_share.1 = (f32[304,2432]{1,0:T(8,128)S(1)}, bf16[608,512]{1,0:T(8,128)(2,1)S(1)}, f32[2,2432,128]{2,1,0:T(8,128)S(1)}, f32[4,80,128]{2,1,0:T(8,128)S(1)}) custom-call(bf16[64,32768]{1,0:T(8,128)(2,1)} %snap_hbm.1, bf16[68,32768]{1,0:T(8,128)(2,1)} %pod_hbm.1, f32[2415]{0:T(1024)} %pen_hbm.1), custom_call_target="tpu_custom_call" | custom-call | tf_op jit(solution)/shard_map/project_and_share/pallas_call | solution.py:231
  26.4 2.7 %normal_equations.1 = (f32[302,2415]{1,0:T(8,128)}, f32[68,302]{1,0:T(8,128)}, f32[1,2,68]{2,1,0:T(2,128)}, f32[1,2,68]{2,1,0:T(2,128)}) custom-call(f32[304,2432]{1,0:T(8,128)S(1)} %get-tuple-element.12.part_ref, bf16[608,512]{1,0:T(8,128)(2,1)S(1)} %get-tuple-element.13.own_ref, f32[2,2432,128]{2,1,0:T(8,128)S(1)} %get-tuple-element.14.late_ref, ...), custom_call_target="tpu_custom_call" | custom-call | tf_op jit(solution)/shard_map/normal_equations/pallas_call | solution.py:259

commit v5 on v4

--- a/solution.py
+++ b/solution.py
@@ -14,7 +14,7 @@
 PAD = -(-OWN // 16) * 16
 GROUPS = 4
 NX, NZ, NT = 4, 8, 8
-CHUNKS = (2048, 6144, 6144, 6144, 4096, 4096, 2048, 1024, 1024)
+CHUNKS = (1024, 2048) + (3072,) * 9 + (1024, 512, 512)
 SLOTS = (0, 1, 3, 2)
 LAST = 2432
 MESH = pl.DeviceIdType.MESH
@@ -60,11 +60,12 @@
     space, tm = lax.axis_index("space"), lax.axis_index("tm")
     z, x = space // NX, lax.rem(space, NX)
     y, core = tm // 2, lax.rem(tm, 2)
-    x_peers = [(z * NX + lax.rem(x + k, NX), tm) for k in (2, 1, 3)]
-    z_peers = [(lax.rem(z + k, NZ) * NX + x, tm) for k in (4, 3, 5, 2, 6, 1, 7)]
+    x_peers = [(z * NX + k + (x <= k).astype(jnp.int32), tm) for k in range(NX - 1)]
+    z_peers = [((k + (z <= k).astype(jnp.int32)) * NX + x, tm) for k in range(NZ - 1)]
     chips = [lax.rem(y + k, GROUPS) for k in range(GROUPS)]
     sibling = (space, 2 * y + (1 - core))
-    t_peers = [sibling] + [(space, 2 * chips[k] + c) for k in range(1, GROUPS) for c in range(2)]
+    y_peers = [k + (y <= k).astype(jnp.int32) for k in range(GROUPS - 1)]
+    t_peers = [sibling] + [(space, 2 * chip + c) for chip in y_peers for c in range(2)]
 
     loads, at = [], 0
     for i, width in enumerate(CHUNKS):
@@ -99,11 +100,11 @@
 
     pl.semaphore_wait(barrier, len(peers))
 
-    def send(buf, rank, peer, phase):
+    def send(buf, rank, peer, way, phase):
         pltpu.make_async_remote_copy(
             src_ref=buf.at[rank],
             dst_ref=buf.at[rank],
-            send_sem=send_sem.at[min(phase, 2)],
+            send_sem=send_sem.at[way],
             recv_sem=recv_sem.at[phase],
             device_id=peer,
             device_id_type=MESH,
@@ -115,19 +116,19 @@
 
     xbuf[x] = packed
     for peer in x_peers:
-        send(xbuf, x, peer, 0)
+        send(xbuf, x, peer, 0, 0)
     arrived(xbuf, 0, NX - 1, recv_sem.at[0])
     zbuf[z] = (xbuf[0] + xbuf[1]) + (xbuf[2] + xbuf[3])
     for peer in z_peers:
-        send(zbuf, z, peer, 1)
+        send(zbuf, z, peer, 1, 1)
     arrived(zbuf, 0, NZ - 1, recv_sem.at[1])
     tbuf[tm] = ((zbuf[0] + zbuf[1]) + (zbuf[2] + zbuf[3])) + (
         (zbuf[4] + zbuf[5]) + (zbuf[6] + zbuf[7])
     )
-    send(tbuf, tm, sibling, 2)
-    for k in SLOTS[1:]:
+    send(tbuf, tm, sibling, 2, 2)
+    for chip in y_peers:
         for c in range(2):
-            send(tbuf, tm, (space, 2 * chips[GROUPS - k] + c), 2 + k)
+            send(tbuf, tm, (space, 2 * chip + c), 2, 2 + lax.rem(y - chip + GROUPS, GROUPS))
 
     half_lane = lax.broadcasted_iota(jnp.int32, (HALF, 128), 1) < 64
     first_row = tm * OWN
@@ -169,8 +170,8 @@
     arrived(tbuf, 2 * chips[2], 2, recv_sem.at[4])
     build(3)
 
-    for phase, (buf, count) in enumerate(((xbuf, NX - 1), (zbuf, NZ - 1), (tbuf, NT - 1))):
-        arrived(buf, 0, count, send_sem.at[phase])
+    for way, buf, count in ((0, xbuf, NX - 1), (1, zbuf, NZ - 1), (2, tbuf, NT - 1)):
+        arrived(buf, 0, count, send_sem.at[way])
 
 
 def place(feat, late_ref, g, rows, value):

time: 29.1 us -> 28.5 us (0.979)
  Pallas kernels: 28.4 us -> 27.8 us
    pallas_call x1, Pallas kernels: 25.7 us -> 25.2 us  [shards(): pl.pallas_call(project_and_share, out_shape=[pltpu.VMEM((PAD, LAST), jnp....]
where the time goes in v5:
time: 28.5 us
  Pallas kernels  27.8 us (98%)
  between operations  0.64 us (2%)
    pallas_call x1, Pallas kernels, shards(): pl.pallas_call(project_and_share, out_shape=[pltpu.VMEM((PAD, LAST), jnp....  25.2 us
    pallas_call x1, Pallas kernels, shards(): pl.pallas_call(normal_equations, out_shape=[jax.ShapeDtypeStruct((OWN, F)...  2.65 us

profile of v5, /device:TPU:1, one launch (start us, length us, event | category | flops | bytes accessed | tf_op | source)
XLA Modules:
  0.0 28.5 jit_solution(10644971045068918078)
XLA Ops:
  0.6 25.2 %project_and_share.1 = (f32[304,2432]{1,0:T(8,128)S(1)}, bf16[608,512]{1,0:T(8,128)(2,1)S(1)}, f32[2,2432,128]{2,1,0:T(8,128)S(1)}, f32[4,80,128]{2,1,0:T(8,128)S(1)}) custom-call(bf16[64,32768]{1,0:T(8,128)(2,1)} %snap_hbm.1, bf16[68,32768]{1,0:T(8,128)(2,1)} %pod_hbm.1, f32[2415]{0:T(1024)} %pen_hbm.1), custom_call_target="tpu_custom_call" | custom-call | tf_op jit(solution)/shard_map/project_and_share/pallas_call | solution.py:232
  25.8 2.7 %normal_equations.1 = (f32[302,2415]{1,0:T(8,128)}, f32[68,302]{1,0:T(8,128)}, f32[1,2,68]{2,1,0:T(2,128)}, f32[1,2,68]{2,1,0:T(2,128)}) custom-call(f32[304,2432]{1,0:T(8,128)S(1)} %get-tuple-element.12.part_ref, bf16[608,512]{1,0:T(8,128)(2,1)S(1)} %get-tuple-element.13.own_ref, f32[2,2432,128]{2,1,0:T(8,128)S(1)} %get-tuple-element.14.late_ref, ...), custom_call_target="tpu_custom_call" | custom-call | tf_op jit(solution)/shard_map/normal_equations/pallas_call | solution.py:260

commit v6 on v5

--- a/solution.py
+++ b/solution.py
@@ -57,6 +57,19 @@
     snap_hbm, pod_hbm, pen_hbm, part_ref, own_ref, late_ref, modes,
     snap, pod, pen, xbuf, zbuf, tbuf, feat, load_sem, pen_sem, send_sem, recv_sem
 ):
+    loads, at = [], 0
+    for i, width in enumerate(CHUNKS):
+        cols = slice(at, at + width)
+        at += width
+        loads.append((
+            cols,
+            pltpu.make_async_copy(snap_hbm.at[:, cols], snap.at[:, cols], load_sem.at[0, i]),
+            pltpu.make_async_copy(pod_hbm.at[:, cols], pod.at[:, cols], load_sem.at[1, i]),
+        ))
+    for _, first, second in loads[:5]:
+        first.start()
+        second.start()
+
     space, tm = lax.axis_index("space"), lax.axis_index("tm")
     z, x = space // NX, lax.rem(space, NX)
     y, core = tm // 2, lax.rem(tm, 2)
@@ -67,25 +80,16 @@
     y_peers = [k + (y <= k).astype(jnp.int32) for k in range(GROUPS - 1)]
     t_peers = [sibling] + [(space, 2 * chip + c) for chip in y_peers for c in range(2)]
 
-    loads, at = [], 0
-    for i, width in enumerate(CHUNKS):
-        cols = slice(at, at + width)
-        at += width
-        loads.append((
-            cols,
-            pltpu.make_async_copy(snap_hbm.at[:, cols], snap.at[:, cols], load_sem.at[0, i]),
-            pltpu.make_async_copy(pod_hbm.at[:, cols], pod.at[:, cols], load_sem.at[1, i]),
-        ))
-    for _, first, second in loads:
+    barrier = pltpu.get_barrier_semaphore()
+    peers = z_peers + t_peers + x_peers
+    for peer in peers:
+        pl.semaphore_signal(barrier, inc=1, device_id=peer, device_id_type=MESH)
+
+    for _, first, second in loads[5:]:
         first.start()
         second.start()
     pen_copy = pltpu.make_async_copy(pen_hbm, pen, pen_sem)
     pen_copy.start()
-
-    barrier = pltpu.get_barrier_semaphore()
-    peers = z_peers + t_peers + x_peers
-    for peer in peers:
-        pl.semaphore_signal(barrier, inc=1, device_id=peer, device_id_type=MESH)
 
     for g in range(GROUPS):
         place(feat, late_ref, g, slice(0, 1), jnp.ones((1, 128), jnp.float32))

time: 28.5 us -> 28.6 us (level)
  no operation moved by 1% of the time
where the time goes in v6:
time: 28.6 us; the launch traced here: 28.5 us
  Pallas kernels  27.8 us (97%)
  between operations  0.64 us (2%)
    pallas_call x1, Pallas kernels, shards(): pl.pallas_call(project_and_share, out_shape=[pltpu.VMEM((PAD, LAST), jnp....  25.2 us
    pallas_call x1, Pallas kernels, shards(): pl.pallas_call(normal_equations, out_shape=[jax.ShapeDtypeStruct((OWN, F)...  2.65 us

profile of v6, /device:TPU:1, one launch (start us, length us, event | category | flops | bytes accessed | tf_op | source)
XLA Modules:
  0.0 28.5 jit_solution(7273744620180159809)
XLA Ops:
  0.6 25.2 %project_and_share.1 = (f32[304,2432]{1,0:T(8,128)S(1)}, bf16[608,512]{1,0:T(8,128)(2,1)S(1)}, f32[2,2432,128]{2,1,0:T(8,128)S(1)}, f32[4,80,128]{2,1,0:T(8,128)S(1)}) custom-call(bf16[64,32768]{1,0:T(8,128)(2,1)} %snap_hbm.1, bf16[68,32768]{1,0:T(8,128)(2,1)} %pod_hbm.1, f32[2415]{0:T(1024)} %pen_hbm.1), custom_call_target="tpu_custom_call" | custom-call | tf_op jit(solution)/shard_map/project_and_share/pallas_call | solution.py:236
  25.8 2.6 %normal_equations.1 = (f32[302,2415]{1,0:T(8,128)}, f32[68,302]{1,0:T(8,128)}, f32[1,2,68]{2,1,0:T(2,128)}, f32[1,2,68]{2,1,0:T(2,128)}) custom-call(f32[304,2432]{1,0:T(8,128)S(1)} %get-tuple-element.12.part_ref, bf16[608,512]{1,0:T(8,128)(2,1)S(1)} %get-tuple-element.13.own_ref, f32[2,2432,128]{2,1,0:T(8,128)S(1)} %get-tuple-element.14.late_ref, ...), custom_call_target="tpu_custom_call" | custom-call | tf_op jit(solution)/shard_map/normal_equations/pallas_call | solution.py:264

commit v7 on v6

--- a/solution.py
+++ b/solution.py
@@ -200,11 +200,21 @@
     for n, (at, end) in enumerate(tiles()):
         cols = slice(at, min(end, F))
         value = jnp.concatenate([late_ref[0, at:end], late_ref[1, at:end]], axis=1)
-        gram = pair_products(own, *split(value)) + part_ref[:, at:end]
+        high, low = split(value)
+        if end == LAST:
+            high = jnp.concatenate([high, rate_hi[:, snaps // 2 :]], axis=0)
+            low = jnp.concatenate([low, rate_lo[:, snaps // 2 :]], axis=0)
+            gram = pair_products(own, high, low)
+            rhs = gram[:, end - at :] + rhs_early
+            gram = gram[:, : end - at] + part_ref[:, at:end]
+            rbuf[...] = rhs[:OWN].T[:R]
+            write(rbuf, rhs_ref, len(tiles()))
+        else:
+            gram = pair_products(own, high, low) + part_ref[:, at:end]
         obuf[:, cols] = gram[:OWN, : cols.stop - at]
         write(obuf.at[:, cols], normal_ref.at[:, cols], n)
 
-        if n == 6:
+        if n == 8:
             order = [modes[SLOTS.index(k), :72] for k in range(GROUPS)]
             whole = jnp.concatenate(order, axis=1)
             when = lax.rem(lax.broadcasted_iota(jnp.int32, (72, snaps), 1) + (tm // 2) * 128, snaps)
@@ -221,9 +231,8 @@
             write(mine.at[0], state_ref, len(tiles()) + 1)
             write(mine.at[1], rate_ref, len(tiles()) + 2)
             rate = jnp.concatenate([rate[:, 128 * k : 128 * (k + 1)] for k in SLOTS], axis=1)
-            rhs = pair_products(own_ref[...], *split(rate))
-            rbuf[...] = rhs[:OWN].T[:R]
-            write(rbuf, rhs_ref, len(tiles()))
+            rate_hi, rate_lo = split(rate)
+            rhs_early = pair_products(own_ref[:, : snaps // 2], rate_hi[:, : snaps // 2], rate_lo[:, : snaps // 2])
     for copy in copies:
         copy.wait()
 

time: 28.6 us -> 28.4 us (level)
  no operation moved by 1% of the time
where the time goes in v7:
time: 28.4 us; the launch traced here: 28.3 us
  Pallas kernels  27.7 us (98%)
  between operations  0.64 us (2%)
    pallas_call x1, Pallas kernels, shards(): pl.pallas_call(project_and_share, out_shape=[pltpu.VMEM((PAD, LAST), jnp....  25.2 us
    pallas_call x1, Pallas kernels, shards(): pl.pallas_call(normal_equations, out_shape=[jax.ShapeDtypeStruct((OWN, F)...  2.5 us

profile of v7, /device:TPU:1, one launch (start us, length us, event | category | flops | bytes accessed | tf_op | source)
XLA Modules:
  0.0 28.3 jit_solution(13444988506270374576)
XLA Ops:
  0.6 25.2 %project_and_share.1 = (f32[304,2432]{1,0:T(8,128)S(1)}, bf16[608,512]{1,0:T(8,128)(2,1)S(1)}, f32[2,2432,128]{2,1,0:T(8,128)S(1)}, f32[4,80,128]{2,1,0:T(8,128)S(1)}) custom-call(bf16[64,32768]{1,0:T(8,128)(2,1)} %snap_hbm.1, bf16[68,32768]{1,0:T(8,128)(2,1)} %pod_hbm.1, f32[2415]{0:T(1024)} %pen_hbm.1), custom_call_target="tpu_custom_call" | custom-call | tf_op jit(solution)/shard_map/project_and_share/pallas_call | solution.py:245
  25.8 2.5 %normal_equations.1 = (f32[302,2415]{1,0:T(8,128)}, f32[68,302]{1,0:T(8,128)}, f32[1,2,68]{2,1,0:T(2,128)}, f32[1,2,68]{2,1,0:T(2,128)}) custom-call(f32[304,2432]{1,0:T(8,128)S(1)} %get-tuple-element.12.part_ref, bf16[608,512]{1,0:T(8,128)(2,1)S(1)} %get-tuple-element.13.own_ref, f32[2,2432,128]{2,1,0:T(8,128)S(1)} %get-tuple-element.14.late_ref, ...), custom_call_target="tpu_custom_call" | custom-call | tf_op jit(solution)/shard_map/normal_equations/pallas_call | solution.py:273

commit v8 on v7

--- a/solution.py
+++ b/solution.py
@@ -14,7 +14,7 @@
 PAD = -(-OWN // 16) * 16
 GROUPS = 4
 NX, NZ, NT = 4, 8, 8
-CHUNKS = (1024, 2048) + (3072,) * 9 + (1024, 512, 512)
+CHUNKS = (1024, 3072) + (4096,) * 6 + (2048, 1024, 1024)
 SLOTS = (0, 1, 3, 2)
 LAST = 2432
 MESH = pl.DeviceIdType.MESH

time: 28.4 us -> 28.4 us (level)
  no operation moved by 1% of the time
where the time goes in v8:
time: 28.4 us; the launch traced here: 28.3 us
  Pallas kernels  27.7 us (98%)
  between operations  0.64 us (2%)
    pallas_call x1, Pallas kernels, shards(): pl.pallas_call(project_and_share, out_shape=[pltpu.VMEM((PAD, LAST), jnp....  25.2 us
    pallas_call x1, Pallas kernels, shards(): pl.pallas_call(normal_equations, out_shape=[jax.ShapeDtypeStruct((OWN, F)...  2.51 us

profile of v8, /device:TPU:1, one launch (start us, length us, event | category | flops | bytes accessed | tf_op | source)
XLA Modules:
  0.0 28.3 jit_solution(14223230422744406041)
XLA Ops:
  0.6 25.2 %project_and_share.1 = (f32[304,2432]{1,0:T(8,128)S(1)}, bf16[608,512]{1,0:T(8,128)(2,1)S(1)}, f32[2,2432,128]{2,1,0:T(8,128)S(1)}, f32[4,80,128]{2,1,0:T(8,128)S(1)}) custom-call(bf16[64,32768]{1,0:T(8,128)(2,1)} %snap_hbm.1, bf16[68,32768]{1,0:T(8,128)(2,1)} %pod_hbm.1, f32[2415]{0:T(1024)} %pen_hbm.1), custom_call_target="tpu_custom_call" | custom-call | tf_op jit(solution)/shard_map/project_and_share/pallas_call | solution.py:245
  25.8 2.5 %normal_equations.1 = (f32[302,2415]{1,0:T(8,128)}, f32[68,302]{1,0:T(8,128)}, f32[1,2,68]{2,1,0:T(2,128)}, f32[1,2,68]{2,1,0:T(2,128)}) custom-call(f32[304,2432]{1,0:T(8,128)S(1)} %get-tuple-element.12.part_ref, bf16[608,512]{1,0:T(8,128)(2,1)S(1)} %get-tuple-element.13.own_ref, f32[2,2432,128]{2,1,0:T(8,128)S(1)} %get-tuple-element.14.late_ref, ...), custom_call_target="tpu_custom_call" | custom-call | tf_op jit(solution)/shard_map/normal_equations/pallas_call | solution.py:273
